TPU v7x, 256 devices: a whole 4x4x8 slice. The times are simulated.
256 devices in a mesh: owner: 32 (over x, y, core), aux: 8 (over z).
Axes of the slice: x: 4, y: 4, z: 8, core: 2. Of those that a mesh axis runs over, the one named last changes fastest.
Arguments:
- fit_left: bfloat16 [128, 256, 128, 128], P('owner', 'aux'), may hold values from -0.5 to 0.5
- fit_right: bfloat16 [128, 256, 128, 128], P('owner', 'aux'), may hold values from -0.03125 to 0.03125
- t2_tiles: bfloat16 [128, 8, 128, 128], P('owner'), may hold values from -6 to 6
- task_count: int32 [32], P('owner'), may hold values from 1 to 4, as said below
- task_target: int32 [128], P('owner'), may hold values from 0 to 31
Outputs:
- residual: bfloat16 [32, 8, 128, 128], P('owner', 'aux')
Inputs may be any that keep to these rules, and one draw needn't show every extreme that they name: task_count equals 4 on at least one index of owner.
All inputs are finite; a program needn't handle non-finite values.
Results may differ from a plain program's by a relative error of at most 0.0049.
Values may be sent and summed in bfloat16 or wider, within the bound.
A program may use at most 128 MiB of HBM per device.

v0:
```python
import jax
import jax.numpy as jnp
from jax import lax
from jax.sharding import PartitionSpec as P


def ladder_term(left_fit, right_fit, amplitudes):
    halves = jnp.einsum(
        "qac,icd->qiad", left_fit, amplitudes, preferred_element_type=jnp.float32
    ).astype(jnp.bfloat16)
    return jnp.einsum("qiad,qbd->iab", halves, right_fit, preferred_element_type=jnp.float32)


def store_terms(group, pair_count, tile_width):
    left_fit, right_fit, amplitudes, targets, lower, upper = group
    buffer = jnp.zeros((left_fit.shape[0], pair_count, tile_width, tile_width), jnp.float32)

    def step(position, accum):
        return accum.at[position].set(
            ladder_term(left_fit[position], right_fit[position], amplitudes[position])
        )

    return lax.fori_loop(lower, upper, step, buffer)


def owner_sums(groups, owners, pair_count, tile_width):
    buffers = [store_terms(group, pair_count, tile_width) for group in groups]
    all_terms = buffers[0]
    all_targets = jnp.concatenate([group[3] for group in groups], axis=0)
    shares = lax.psum_scatter(all_terms, "aux", scatter_dimension=1, tiled=True)
    one_hot = (all_targets[None, :] == jnp.arange(owners, dtype=jnp.int32)[:, None]).astype(
        jnp.float32
    )
    return jnp.einsum("nt,tpxy->npxy", one_hot, shares, precision=lax.Precision.HIGHEST)


def on_device(fit_left, fit_right, t2_tiles, task_count, task_target):
    owners = lax.axis_size("owner")
    pair_count = t2_tiles.shape[1]
    tile_width = t2_tiles.shape[2]
    loaded = task_count[0]
    groups = [(fit_left, fit_right, t2_tiles, task_target, 0, loaded)]
    per_owner = owner_sums(groups, owners, pair_count, tile_width)
    summed = lax.psum_scatter(per_owner, "owner", scatter_dimension=0, tiled=True)
    return summed.astype(jnp.bfloat16)


def solution(mesh):
    placed = (
        P("owner", "aux", None, None),
        P("owner", "aux", None, None),
        P("owner", None, None, None),
        P("owner"),
        P("owner"),
    )
    return jax.shard_map(
        on_device,
        mesh=mesh,
        in_specs=placed,
        out_specs=P("owner", "aux", None, None),
        check_vma=False,
    )
```

profile of v0, /device:TPU:1, one launch (start us, length us, event | category | flops | bytes accessed | tf_op | source)
XLA Modules:
  0.0 237.3 jit_solution(1457001532928693600)
XLA Ops:
  6.5 0.0 copy-start.1
  6.5 0.0 all-reduce.3.cloned.1.call-start
  6.5 0.2 broadcast_in_dim.3
  6.8 0.4 copy-done.1
  7.2 11.9 %while.11 = (s32[]{:T(128)}, f32[4,8,128,128]{3,2,1,0:T(8,128)S(1)}, s32[]{:T(128)}, bf16[4,8,128,128]{3,2,1,0:T(8,128)(2,1)}, bf16[4,32,128,128]{3,2,1,0:T(8,12...) while((s32[]{:T(128)}, ...), condition=%wide.region_2.0_spmd, body=%wide.region_0.0_spmd.sunk | while | flops 2151809024 | bytes 3410600 | solution.py:23
  7.9 0.7 and_reduce_fusion.2
  8.6 9.9 %fusion.39 = f32[4,8,128,128]{3,2,1,0:T(8,128)S(1)} fusion(f32[4,8,128,128]{3,2,1,0:T(8,128)S(1)} %get-tuple-element.113, s32[]{:T(128)} %select_n.9, bf16[4,32,128,128]{3,2,1,0:T(8,128)(2,1)} %get-tuple-element.128, bf16[4,32,128,128]{3,2,1,0:T(8,128)(2,1)} %get-tuple-element.127, bf16[4,8,128,128]{3,2,1,0:T(8,128)(2,1)} %get-tuple-element.126, ...), kind=kOutput, calls=%fused_computation.6.clone.1 | convolution fusion | flops 2151809024 | bytes 3410432 | tf_op jit(solution)/shard_map/while/body/qiad,qbd->iab/dot_general | solution.py:11
  19.1 0.0 copy-start
  19.1 0.0 copy-start.3
  19.2 0.0 copy-start.2
  19.2 1.3 copy-done
  20.4 0.0 all-reduce.3.cloned.1.call-update
  20.5 0.0 reduce-scatter.5.cloned.1.call-start
  20.5 0.0 copy-done.3
  20.5 0.6 dynamic-slice.10
  21.1 115.8 %all-reduce.3.cloned.1.call-done = f32[4,8,128,128]{3,2,1,0:T(8,128)} async-done(((f32[4,8,128,128]{3,2,1,0:T(8,128)}), f32[4,8,128,128]{3,2,1,0:T(8,128)}) %all-reduce.3.cloned.1.call-update) | async-done | bytes 2097168
  136.9 1.6 dynamic-slice_bitcast_fusion
  138.5 0.0 copy-done.2
  138.5 1.1 convolution_bitcast_fusion
  139.6 2.6 %copy.9 = f32[32,1,128,128]{3,2,1,0:T(8,128)} copy(f32[32,1,128,128]{3,0,2,1:T(8,128)S(1)} %convolution_bitcast_fusion) | data formatting | bytes 4194304 | tf_op jit(solution)/shard_map/nt,tpxy->npxy/dot_general | solution.py:34
  142.2 0.0 reduce-scatter.5.cloned.1.call-update
  142.2 86.7 %reduce-scatter.5.cloned.1.call-done = f32[1,1,128,128]{3,2,1,0:T(8,128)} async-done(((f32[32,1,128,128]{3,2,1,0:T(8,128)}), f32[1,1,128,128]{3,2,1,0:T(8,128)}) %reduce-scatter.5.cloned.1.call-update) | async-done | bytes 65552 | tf_op jit(solution)/shard_map/reduce_scatter | solution.py:44
  229.0 1.5 convert_element_type.10
Async XLA Ops:
  6.5 0.7 copy-start.1
  6.5 130.4 %all-reduce.3.cloned.1.call-start = ((), (), s32[]{:S(2)}) async-start(), calls=%async_computation.2 | async-start | bytes 4194304
  19.1 1.3 copy-start
  19.1 1.4 copy-start.3
  19.2 119.4 %copy-start.2 = (s32[4]{0:T(128)S(1)}, s32[4]{0:T(128)}, u32[]{:S(2)}) copy-start(s32[4]{0:T(128)} %param.13) | copy-start | bytes 52
  20.5 208.5 %reduce-scatter.5.cloned.1.call-start = ((), (), s32[]{:S(2)}) async-start(), calls=%async_computation.1 | async-start | bytes 2162688 | tf_op jit(solution)/shard_map/reduce_scatter | solution.py:44
Sparse Core Ops, SparseCore 0:
  20.6 116.2 all-reduce.2
  142.3 86.5 reduce-scatter.4
where the time goes:
time: 238 us; the launch traced here: 237 us
  waiting for transfers between devices  203 us (85%)
  between operations  13.5 us (6%)
  matrix products  11 us (5%)
  local copies, waits for them, and re-layouts  6.69 us (3%)
    unnamed x3, waiting for transfers between devices  116 us
    reduce_scatter x1, waiting for transfers between devices, on_device(): lax.psum_scatter(per_owner, 'owner', scatter_dimension=0, tiled=True)  86.7 us
    dot_general x1, matrix products, ladder_term(): jnp.einsum('qiad,qbd->iab', halves, right_fit, preferred_element_type=jnp...  9.87 us
  transfers between devices with their start and end apart: 2, of which 2 were waited for; matrix products, arithmetic and copies ran while one was open for 0% of the time, Pallas kernels for 0%

commit v1 on v0

v1 whole, which is shorter than its diff:
```python
import functools

import jax
import jax.numpy as jnp
from jax import lax
from jax.experimental import pallas as pl
from jax.experimental.pallas import tpu as pltpu
from jax.sharding import PartitionSpec as P

MESH = pl.DeviceIdType.MESH
f32, bf16 = jnp.float32, jnp.bfloat16
FAR = (4, 3, 5, 1)
NEAR = (2, 6, 7, 0)


def kernel(
    sizes, count_ref, target_ref, left_hbm, right_hbm, t2_hbm, out_ref,
    left, right, t2, half, term, far_out, relay, relay_info, near_out, near_in, info, own, blocks_out, blocks_in,
    load_sem, far_send, relay_recv, near_send, near_recv, info_send, info_recv, block_send, block_recv,
):
    owners, aux, parts, tasks, naux, tile = sizes
    rows = tile // parts
    me = lax.axis_index("owner")
    z = lax.axis_index("aux")
    part = lax.rem(me, parts)

    def at(dz, m):
        return ((me // parts) * parts + lax.rem(part + m, parts), lax.rem(z + dz, aux))

    def loads(g):
        return [
            pltpu.make_async_copy(t2_hbm.at[g], t2.at[g], load_sem.at[0, g]),
            pltpu.make_async_copy(left_hbm.at[g], left.at[g], load_sem.at[1, g]),
            pltpu.make_async_copy(right_hbm.at[g], right.at[g], load_sem.at[2, g]),
        ]

    for g in range(tasks):
        for copy in loads(g):
            copy.start()

    barrier = pltpu.get_barrier_semaphore()
    for dz in (1, 2, 6, 7):
        for m in range(parts):
            pl.semaphore_signal(barrier, inc=1, device_id=at(dz, m), device_id_type=MESH)

    def greet(r, carry):
        pl.semaphore_signal(
            barrier, inc=1, device_id=(lax.rem(me + r, owners), z), device_id_type=MESH
        )
        return carry

    lax.fori_loop(1, owners, greet, 0)

    rows_of_info = [
        jnp.full((1, tile), jnp.where(g < count_ref[0], target_ref[g], -1), jnp.int32)
        for g in range(tasks)
    ]
    info[0] = jnp.concatenate(rows_of_info + [jnp.full((8 - tasks, tile), -1, jnp.int32)], axis=0)

    def info_copy(m):
        return pltpu.make_async_remote_copy(
            src_ref=info.at[0], dst_ref=info.at[m], send_sem=info_send.at[m], recv_sem=info_recv.at[m],
            device_id=at(0, m), device_id_type=MESH,
        )

    def relay_copy(p, g):
        dz = (2 + 4 * (g // 2), 1, 7)[p]
        return pltpu.make_async_remote_copy(
            src_ref=far_out.at[p, g], dst_ref=relay.at[p, g], send_sem=far_send.at[p, g],
            recv_sem=relay_recv.at[p, g], device_id=at(dz, 0), device_id_type=MESH,
        )

    def near_copy(s, m, g):
        dz = (1, 2, 6, 7, 0)[s]
        away = lax.rem(part + m, parts)
        return pltpu.make_async_remote_copy(
            src_ref=near_out.at[s, g, pl.ds(pl.multiple_of(away * rows, rows), rows)],
            dst_ref=near_in.at[s, m, g], send_sem=near_send.at[s, m, g],
            recv_sem=near_recv.at[s, m, g], device_id=at(dz, m), device_id_type=MESH,
        )

    def block_copy(r):
        return pltpu.make_async_remote_copy(
            src_ref=blocks_out.at[r], dst_ref=blocks_in.at[r], send_sem=block_send.at[r],
            recv_sem=block_recv.at[r], device_id=(lax.rem(me + r, owners), z), device_id_type=MESH,
        )

    def multiply(g, near):
        pairs = [lax.rem(z + FAR[p] + near * (NEAR[p] - FAR[p] + aux), aux) for p in range(4)]
        amps = jnp.concatenate([t2[g, pair].T for pair in pairs], axis=0)
        step = 8
        for q in range(0, naux, step):
            block = lax.dot_general(
                amps, left[g, q : q + step].reshape(step * tile, tile), (((1,), (1,)), ((), ())),
                preferred_element_type=f32,
            ).astype(bf16)
            for k in range(step):
                for p in range(4):
                    half[(q + k) * tile : (q + k + 1) * tile, p * tile : (p + 1) * tile] = block[
                        p * tile : (p + 1) * tile, k * tile : (k + 1) * tile
                    ]
        fit = jnp.concatenate([right[g, q] for q in range(naux)], axis=1)
        term[...] = jnp.dot(fit, half[...], preferred_element_type=f32)

    def block_of(p):
        return term[:, p * tile : (p + 1) * tile]

    def send_near(s, g, value):
        near_out[s, g] = value.astype(bf16)
        for m in range(parts):
            if s < 4 or m:
                near_copy(s, m, g).start()

    def unit(u, carry):
        near = u // tasks
        g = lax.rem(u, tasks)

        @pl.when(near == 0)
        def _():
            for copy in loads(g):
                copy.wait()

        multiply(g, near)

        @pl.when(u == 0)
        def _():
            pl.semaphore_wait(barrier, 4 * parts + owners - 1)
            for m in range(1, parts):
                info_copy(m).start()

        @pl.when(near == 0)
        def _():
            for p in range(3):
                far_out[p, g] = block_of(p).astype(bf16)
                relay_copy(p, g).start()
            send_near(0, g, block_of(3))

        @pl.when(near == 1)
        def _():
            for p in range(3):
                relay_copy(p, g).wait_recv()
            extra = relay[0, g].astype(f32)
            up = (g // 2 == 0).astype(f32)
            send_near(1, g, block_of(0) + relay[1, g].astype(f32) + extra * up)
            send_near(2, g, block_of(1) + relay[2, g].astype(f32) + extra * (1.0 - up))
            send_near(3, g, block_of(2))
            send_near(4, g, block_of(3))
            own[g] = term[pl.ds(pl.multiple_of(part * rows, rows), rows), 3 * tile :]

        return carry

    lax.fori_loop(0, 2 * tasks, unit, 0)

    for m in range(1, parts):
        info_copy(m).wait_recv()

    def drain(g, carry):
        for m in range(parts):
            for s in range(5):
                if s < 4 or m:
                    near_copy(s, m, g).wait_recv()
                    value = near_in[s, m, g].astype(f32)
                    total = value if s == 0 else total + value
            if m == 0:
                total = total + own[g]
            relay_info[m, g] = total
        return carry

    lax.fori_loop(0, tasks, drain, 0)

    def gather(r):
        target = lax.rem(me + r, owners)
        total = jnp.zeros((rows, tile), f32)
        for m in range(parts):
            for g in range(tasks):
                hit = jnp.broadcast_to(info[m, g : g + 1, :], (rows, tile)) == target
                total += jnp.where(hit, relay_info[m, g], 0.0)
        return total

    def scatter(r, carry):
        blocks_out[r] = gather(r).astype(bf16)
        block_copy(r).start()
        return carry

    lax.fori_loop(1, owners, scatter, 0)
    term[:, 0:tile] = jnp.zeros((tile, tile), f32)
    term[pl.ds(pl.multiple_of(part * rows, rows), rows), 0:tile] = gather(0)

    def collect(r, carry):
        block_copy(r).wait_recv()
        source = lax.rem(lax.rem(me + owners - r, owners), parts)
        where = pl.ds(pl.multiple_of(source * rows, rows), rows)
        term[where, 0:tile] += blocks_in[r].astype(f32)
        return carry

    lax.fori_loop(1, owners, collect, 0)
    out_ref[0, 0] = term[:, 0:tile].T.astype(bf16)

    for m in range(1, parts):
        info_copy(m).wait_send()

    def finish(g, carry):
        for p in range(3):
            relay_copy(p, g).wait_send()
        for s in range(5):
            for m in range(parts):
                if s < 4 or m:
                    near_copy(s, m, g).wait_send()
        return carry

    lax.fori_loop(0, tasks, finish, 0)

    def finish_blocks(r, carry):
        block_copy(r).wait_send()
        return carry

    lax.fori_loop(1, owners, finish_blocks, 0)


def solution(mesh):
    owners, aux = mesh.shape["owner"], mesh.shape["aux"]
    parts = 2

    def on_device(fit_left, fit_right, t2_tiles, task_count, task_target):
        tasks, naux, tile, _ = fit_left.shape
        pairs = t2_tiles.shape[1]
        rows = tile // parts
        vmem, dma = pltpu.VMEM, pltpu.SemaphoreType.DMA
        return pl.pallas_call(
            functools.partial(kernel, (owners, aux, parts, tasks, naux, tile)),
            out_shape=jax.ShapeDtypeStruct((1, 1, tile, tile), bf16),
            in_specs=[pl.BlockSpec(memory_space=pltpu.SMEM)] * 2 + [pl.BlockSpec(memory_space=pl.ANY)] * 3,
            out_specs=pl.BlockSpec(memory_space=pltpu.VMEM),
            scratch_shapes=[
                vmem((tasks, naux, tile, tile), bf16),
                vmem((tasks, naux, tile, tile), bf16),
                vmem((tasks, pairs, tile, tile), bf16),
                vmem((naux * tile, 4 * tile), bf16),
                vmem((tile, 4 * tile), f32),
                vmem((3, tasks, tile, tile), bf16),
                vmem((3, tasks, tile, tile), bf16),
                vmem((parts, tasks, rows, tile), f32),
                vmem((5, tasks, tile, tile), bf16),
                vmem((5, parts, tasks, rows, tile), bf16),
                vmem((parts, 8, tile), jnp.int32),
                vmem((tasks, rows, tile), f32),
                vmem((owners, rows, tile), bf16),
                vmem((owners, rows, tile), bf16),
                dma((3, tasks)),
                dma((3, tasks)),
                dma((3, tasks)),
                dma((5, parts, tasks)),
                dma((5, parts, tasks)),
                dma((parts,)),
                dma((parts,)),
                dma((owners,)),
                dma((owners,)),
            ],
            compiler_params=pltpu.CompilerParams(
                collective_id=0, has_side_effects=True, vmem_limit_bytes=48 << 20
            ),
            name="ladder",
        )(task_count, task_target, fit_left, fit_right, t2_tiles)

    placed = (
        P("owner", "aux", None, None),
        P("owner", "aux", None, None),
        P("owner", None, None, None),
        P("owner"),
        P("owner"),
    )
    return jax.shard_map(
        on_device,
        mesh=mesh,
        in_specs=placed,
        out_specs=P("owner", "aux", None, None),
        check_vma=False,
    )
```

time: 238 us -> 45.7 us (0.19)
  waiting for transfers between devices: 203 us -> 0 us
  Pallas kernels: 0 us -> 40.1 us
  between operations: 13.5 us -> 0.67 us
  matrix products: 11 us -> 0 us
    unnamed x3 -> x0, waiting for transfers between devices: 116 us -> none
    reduce_scatter x1 -> x0, waiting for transfers between devices: 86.7 us -> none  [on_device(): lax.psum_scatter(per_owner, 'owner', scatter_dimension=0, tiled=True)]
    pallas_call x0 -> x1, Pallas kernels: none -> 40.1 us  [on_device(): pl.pallas_call(functools.partial(kernel, (owners, aux, parts, tasks, naux...]
    dot_general x2 -> x0, matrix products: 11 us -> none  [the longest x1 9.87 us: ladder_term(): jnp.einsum('qiad,qbd->iab', halves, right_fit, preferred_element_type=jnp...]
    dot_general x1 -> x0, local copies, waits for them, and re-layouts: 2.55 us -> none  [owner_sums(): jnp.einsum('nt,tpxy->npxy', one_hot, shares, precision=lax.Precision.HIGH...]
    unnamed x9 -> x7, local copies, waits for them, and re-layouts: 2.29 us -> 4.68 us
  transfers between devices with their start and end apart: 2 -> 0, of which waited for: 2 -> 0; matrix products, arithmetic and copies ran while one was open for 0% -> 0% of each run, Pallas kernels for 0% -> 0%
where the time goes in v1:
time: 45.7 us; the launch traced here: 45.5 us
  Pallas kernels  40.1 us (88%)
  local copies, waits for them, and re-layouts  4.68 us (10%)
  between operations  0.67 us (1%)
    pallas_call x1, Pallas kernels, on_device(): pl.pallas_call(functools.partial(kernel, (owners, aux, parts, tasks, naux...  40.1 us
    unnamed x7, local copies, waits for them, and re-layouts  4.68 us

profile of v1, /device:TPU:1, one launch (start us, length us, event | category | flops | bytes accessed | tf_op | source)
XLA Modules:
  0.0 45.5 jit_solution(15694815791829621885)
XLA Ops:
  0.7 0.0 copy-start
  0.7 2.2 %copy-done = bf16[4,32,128,128]{3,2,1,0:T(8,128)(2,1)S(1)} copy-done((bf16[4,32,128,128]{3,2,1,0:T(8,128)(2,1)S(1)}, bf16[4,32,128,128]{3,2,1,0:T(8,128)(2,1)}, u32[]{:S(2)}) %copy-start) | copy-done | bytes 4194328
  2.8 0.0 copy-start.1
  2.8 1.2 %copy-done.1 = bf16[4,8,128,128]{3,2,1,0:T(8,128)(2,1)S(1)} copy-done((bf16[4,8,128,128]{3,2,1,0:T(8,128)(2,1)S(1)}, bf16[4,8,128,128]{3,2,1,0:T(8,128)(2,1)}, u32[]{:S(2)}) %copy-start.1) | copy-done | bytes 1048600
  4.1 0.0 copy-start.2
  4.1 0.7 %copy-done.2 = s32[4]{0:T(128)S(1)} copy-done((s32[4]{0:T(128)S(1)}, s32[4]{0:T(128)}, u32[]{:S(2)}) %copy-start.2) | copy-done | bytes 40
  4.7 40.1 %ladder.1 = bf16[1,1,128,128]{3,2,1,0:T(8,128)(2,1)S(1)} custom-call(s32[1]{0:T(128)S(6)} %copy.7.count_ref, s32[4]{0:T(128)S(1)} %copy-done.2, bf16[4,32,128,128]{3,2,1,0:T(8,128)(2,1)S(1)} %copy-done, bf16[4,32,128,128]{3,2,1,0:T(8,128)(2,1)} %right_hbm.1, bf16[4,8,128,128]{3,2,1,0:T(8,128)(2,1)S(1)} %copy-done.1), custom_call_target="tpu_custom_call" | custom-call | tf_op jit(solution)/shard_map/ladder/pallas_call | solution.py:229
  44.9 0.6 %copy.8 = bf16[1,1,128,128]{3,2,1,0:T(8,128)(2,1)} copy(bf16[1,1,128,128]{3,2,1,0:T(8,128)(2,1)S(1)} %ladder.1) | data formatting | bytes 65536
Async XLA Ops:
  0.7 2.2 %copy-start = (bf16[4,32,128,128]{3,2,1,0:T(8,128)(2,1)S(1)}, bf16[4,32,128,128]{3,2,1,0:T(8,128)(2,1)}, u32[]{:S(2)}) copy-start(bf16[4,32,128,128]{3,2,1,0:T(8,128)(2,1)} %left_hbm.1) | copy-start | bytes 12582916
  2.8 1.2 %copy-start.1 = (bf16[4,8,128,128]{3,2,1,0:T(8,128)(2,1)S(1)}, bf16[4,8,128,128]{3,2,1,0:T(8,128)(2,1)}, u32[]{:S(2)}) copy-start(bf16[4,8,128,128]{3,2,1,0:T(8,128)(2,1)} %t2_hbm.1) | copy-start | bytes 3145732
  4.1 0.7 %copy-start.2 = (s32[4]{0:T(128)S(1)}, s32[4]{0:T(128)}, u32[]{:S(2)}) copy-start(s32[4]{0:T(128)} %target_ref.1) | copy-start | bytes 52

commit v2 on v0

v2 whole, which is shorter than its diff:
```python
import functools

import jax
import jax.numpy as jnp
from jax import lax
from jax.experimental import pallas as pl
from jax.experimental.pallas import tpu as pltpu
from jax.sharding import PartitionSpec as P

MESH = pl.DeviceIdType.MESH
f32, bf16 = jnp.float32, jnp.bfloat16
SIDE, CORES, PARTS, CHUNK = 4, 2, 4, 4
OFFSETS = ((4, 3), (5, 1), (2, 6), (7, 0))
NEAR_DZ = (1, 2, 6, 7, 0)
HOLD = 2


def kernel(
    sizes, count_ref, target_ref, left_hbm, right_hbm, t2_hbm, out_ref,
    left, right, t2, half_even, half_odd, term, far_out, relay, near_out, near_in, info, own, blocks, blocks_out,
    blocks_in, total,
    load_sem, left_sem, far_send, relay_recv, near_send, near_recv, info_send, info_recv, block_send, block_recv,
):
    owners, aux, tasks, naux, tile = sizes
    rows = tile // PARTS
    units = tasks * len(OFFSETS)
    slots = owners // PARTS
    me = lax.axis_index("owner")
    z = lax.axis_index("aux")
    x, y, core = me // (SIDE * CORES), lax.rem(me // CORES, SIDE), lax.rem(me, CORES)
    part = core + CORES * lax.rem(x, 2)

    def at(dz, m):
        away = lax.rem(part + m, PARTS)
        there = ((x // 2) * 2 + away // CORES) * (SIDE * CORES) + y * CORES + lax.rem(away, CORES)
        return (there, lax.rem(z + dz, aux))

    def owner_at(m, k):
        dx, dy, dc = 2 * (k // SIDE) + m // CORES, lax.rem(k, SIDE), m % CORES
        return (
            lax.rem(x + dx, SIDE) * (SIDE * CORES) + lax.rem(y + dy, SIDE) * CORES + lax.rem(core + dc, CORES)
        )

    def load_t2(g):
        return pltpu.make_async_copy(t2_hbm.at[g], t2.at[g], load_sem.at[0, g])

    def load_right(g):
        return pltpu.make_async_copy(right_hbm.at[g], right.at[g], load_sem.at[1, g])

    def load_left(g, k):
        part_of = pl.ds(k * (naux // 4), naux // 4)
        return pltpu.make_async_copy(left_hbm.at[g, part_of], left.at[g, part_of], left_sem.at[g, k])

    def start_loads(g):
        load_t2(g).start()
        for k in range(4):
            load_left(g, k).start()
        load_right(g).start()

    start_loads(0)

    barrier = pltpu.get_barrier_semaphore()
    for dz in (1, 2, 6, 7):
        for m in range(PARTS):
            pl.semaphore_signal(barrier, inc=1, device_id=at(dz, m), device_id_type=MESH)

    def greet(r, carry):
        pl.semaphore_signal(
            barrier, inc=1, device_id=(lax.rem(me + r, owners), z), device_id_type=MESH
        )
        return carry

    lax.fori_loop(1, owners, greet, 0)

    rows_of_info = [
        jnp.full((1, tile), jnp.where(g < count_ref[0], target_ref[g], -1), jnp.int32)
        for g in range(tasks)
    ]
    info[0] = jnp.concatenate(rows_of_info + [jnp.full((8 - tasks, tile), -1, jnp.int32)], axis=0)

    def info_copy(m):
        return pltpu.make_async_remote_copy(
            src_ref=info.at[0], dst_ref=info.at[m], send_sem=info_send.at[m], recv_sem=info_recv.at[m],
            device_id=at(0, m), device_id_type=MESH,
        )

    def relay_copy(p, g):
        dz = (2 + 4 * lax.rem(g, 2), 1, 7)[p]
        return pltpu.make_async_remote_copy(
            src_ref=far_out.at[p, g], dst_ref=relay.at[p, g], send_sem=far_send.at[p, g],
            recv_sem=relay_recv.at[p, g], device_id=at(dz, 0), device_id_type=MESH,
        )

    def near_copy(s, m, g):
        away = lax.rem(part + m, PARTS)
        return pltpu.make_async_remote_copy(
            src_ref=near_out.at[s, g, pl.ds(pl.multiple_of(away * rows, rows), rows)],
            dst_ref=near_in.at[s, m, g], send_sem=near_send.at[s, m, g],
            recv_sem=near_recv.at[s, m, g], device_id=at(NEAR_DZ[s], m), device_id_type=MESH,
        )

    def block_copy(m, k):
        return pltpu.make_async_remote_copy(
            src_ref=blocks_out.at[m, k], dst_ref=blocks_in.at[m, k], send_sem=block_send.at[m, k],
            recv_sem=block_recv.at[m, k], device_id=(owner_at(m, k), z), device_id_type=MESH,
        )

    def place(u):
        late, i = u // (2 * tasks), lax.rem(u, 2 * tasks)
        last, j = i // tasks, lax.rem(i, tasks)
        g_late = (1 - last) * (i // 2) + last * (2 + lax.rem(j, 2))
        stage_late = (1 - last) * (3 - lax.rem(i, 2)) + last * (2 + j // 2)
        g = (1 - late) * (u // 2) + late * g_late
        stage = (1 - late) * lax.rem(u, 2) + late * stage_late
        return g, stage

    def amplitudes(u):
        g, stage = place(u)
        found = []
        for p in range(2):
            a, b, c, d = (pair[p] for pair in OFFSETS)
            low = a + stage * (b - a)
            high = c + (stage - 2) * (d - c)
            offset = low + (stage // 2) * (high - low)
            found.append(t2[g, lax.rem(z + offset, aux)].T)
        return jnp.concatenate(found, axis=0)

    def first(half, u, amps, q):
        g, _ = place(u)
        block = lax.dot_general(
            amps, left[g, pl.ds(q, CHUNK)].reshape(CHUNK * tile, tile), (((1,), (1,)), ((), ())),
            preferred_element_type=f32,
        ).astype(bf16)
        for k in range(CHUNK):
            for p in range(2):
                half[(q + k) * tile : (q + k + 1) * tile, p * tile : (p + 1) * tile] = block[
                    p * tile : (p + 1) * tile, k * tile : (k + 1) * tile
                ]

    def second(half, u, q):
        g, _ = place(u)
        fit = jnp.concatenate([right[g, q + k] for k in range(CHUNK)], axis=1)
        value = jnp.dot(fit, half[q * tile : (q + CHUNK) * tile, :], preferred_element_type=f32)
        if q == 0:
            term[...] = value
        else:
            term[...] += value

    def multiply(half_new, half_old, u):
        amps = amplitudes(u + 1)
        for q in range(0, naux, CHUNK):
            first(half_new, u + 1, amps, q)
            second(half_old, u, q)

    def send(u, carry):
        g, stage = place(u)

        @pl.when(stage == 0)
        def _():
            relay_copy(0, g).start()
            relay_copy(1, g).start()

        @pl.when(stage == 1)
        def _():
            relay_copy(2, g).start()
            for m in range(PARTS):
                near_copy(0, m, g).start()

        @pl.when(stage == 2)
        def _():
            for m in range(PARTS):
                near_copy(1, m, g).start()
                near_copy(2, m, g).start()

        @pl.when(stage == 3)
        def _():
            for m in range(PARTS):
                near_copy(3, m, g).start()
            for m in range(1, PARTS):
                near_copy(4, m, g).start()

        return carry

    def deliver(u):
        g, stage = place(u)
        lower, upper = slice(0, tile), slice(tile, 2 * tile)

        @pl.when(stage == 0)
        def _():
            far_out[0, g] = term[:, lower].astype(bf16)
            far_out[1, g] = term[:, upper].astype(bf16)

        @pl.when(stage == 1)
        def _():
            far_out[2, g] = term[:, lower].astype(bf16)
            near_out[0, g] = term[:, upper].astype(bf16)

        @pl.when(stage == 2)
        def _():
            for p in range(3):
                relay_copy(p, g).wait_recv()
            extra = relay[0, g].astype(f32)
            up = (lax.rem(g, 2) == 0).astype(f32)
            near_out[1, g] = (term[:, lower] + relay[1, g].astype(f32) + extra * up).astype(bf16)
            near_out[2, g] = (term[:, upper] + relay[2, g].astype(f32) + extra * (1.0 - up)).astype(bf16)

        @pl.when(stage == 3)
        def _():
            near_out[3, g] = term[:, lower].astype(bf16)
            near_out[4, g] = term[:, upper].astype(bf16)
            own[g] = term[pl.ds(pl.multiple_of(part * rows, rows), rows), upper]

        if isinstance(u, int):
            send(u, 0)
        else:
            @pl.when(u == HOLD)
            def _():
                pl.semaphore_wait(barrier, 4 * PARTS + owners - 1)
                for m in range(1, PARTS):
                    info_copy(m).start()
                lax.fori_loop(0, HOLD, send, 0)

            @pl.when(u >= HOLD)
            def _():
                send(u, 0)

    def pair_of_units(v, carry):
        @pl.when(v < tasks)
        def _():
            load_right(v).wait()

        multiply(half_odd, half_even, 2 * v)
        deliver(2 * v)

        @pl.when(v < tasks - 1)
        def _():
            load_t2(v + 1).wait()
            for k in range(4):
                load_left(v + 1, k).wait()

        @pl.when(v < tasks - 2)
        def _():
            start_loads(v + 2)

        multiply(half_even, half_odd, 2 * v + 1)
        deliver(2 * v + 1)
        return carry

    load_t2(0).wait()
    amps = amplitudes(0)
    for q in range(0, naux, CHUNK):
        if q % (naux // 4) == 0:
            load_left(0, q // (naux // 4)).wait()
        if q == naux - naux // 4:
            start_loads(1)
        first(half_even, 0, amps, q)
    lax.fori_loop(0, units // 2 - 1, pair_of_units, 0)
    multiply(half_odd, half_even, units - 2)
    deliver(units - 2)
    for q in range(0, naux, CHUNK):
        second(half_odd, units - 1, q)
    deliver(units - 1)

    for m in range(1, PARTS):
        info_copy(m).wait_recv()

    def shares(g):
        found = []
        for m in range(PARTS):
            for s in range(5):
                if s < 4 or m:
                    near_copy(s, m, g).wait_recv()
        for m in range(PARTS):
            value = own[g] if m == 0 else near_in[4, m, g].astype(f32)
            for s in range(4):
                value += near_in[s, m, g].astype(f32)
            found.append(value)
        return found

    def add_shares(g, found, m, k):
        target = owner_at(m, k)
        value = None
        for n in range(PARTS):
            hit = jnp.broadcast_to(info[n, pl.ds(g, 1), :], (rows, tile)) == target
            part_of = jnp.where(hit, found[n], 0.0)
            value = part_of if value is None else value + part_of
        return value

    order = [(m, k) for k in (6, 5, 7, 4, 2, 1, 3, 0) for m in (2, 3, 1, 0)]

    def accumulate(g, carry):
        found = shares(g)
        for m, k in order:
            blocks[m, k] += add_shares(g, found, m, k)
        return carry

    blocks[...] = jnp.zeros_like(blocks)
    lax.fori_loop(0, tasks - 1, accumulate, 0)
    found = shares(tasks - 1)
    for m, k in order:
        value = blocks[m, k] + add_shares(tasks - 1, found, m, k)
        if m or k:
            blocks_out[m, k] = value.astype(bf16)
            block_copy(m, k).start()
        else:
            blocks[0, 0] = value

    for m in range(PARTS):
        for k in range(slots):
            if m or k:
                block_copy(m, k).wait_recv()
        value = None
        for k in range(slots):
            one = blocks[0, 0] if m == 0 and k == 0 else blocks_in[m, k].astype(f32)
            value = one if value is None else value + one
        source = lax.rem(core + m % CORES, CORES) + CORES * lax.rem(x + m // CORES, 2)
        total[pl.ds(pl.multiple_of(source * rows, rows), rows), :] = value
    out_ref[0, 0] = total[...].T.astype(bf16)

    for m in range(1, PARTS):
        info_copy(m).wait_send()

    def finish(g, carry):
        for p in range(3):
            relay_copy(p, g).wait_send()
        for s in range(5):
            for m in range(PARTS):
                if s < 4 or m:
                    near_copy(s, m, g).wait_send()
        return carry

    lax.fori_loop(0, tasks, finish, 0)
    for m in range(PARTS):
        for k in range(slots):
            if m or k:
                block_copy(m, k).wait_send()


def solution(mesh):
    owners, aux = mesh.shape["owner"], mesh.shape["aux"]

    def on_device(fit_left, fit_right, t2_tiles, task_count, task_target):
        tasks, naux, tile, _ = fit_left.shape
        pairs = t2_tiles.shape[1]
        rows = tile // PARTS
        slots = owners // PARTS
        vmem, dma = pltpu.VMEM, pltpu.SemaphoreType.DMA
        return pl.pallas_call(
            functools.partial(kernel, (owners, aux, tasks, naux, tile)),
            out_shape=jax.ShapeDtypeStruct((1, 1, tile, tile), bf16),
            in_specs=[pl.BlockSpec(memory_space=pltpu.SMEM)] * 2 + [pl.BlockSpec(memory_space=pl.ANY)] * 3,
            out_specs=pl.BlockSpec(memory_space=pltpu.VMEM),
            scratch_shapes=[
                vmem((tasks, naux, tile, tile), bf16),
                vmem((tasks, naux, tile, tile), bf16),
                vmem((tasks, pairs, tile, tile), bf16),
                vmem((naux * tile, 2 * tile), bf16),
                vmem((naux * tile, 2 * tile), bf16),
                vmem((tile, 2 * tile), f32),
                vmem((3, tasks, tile, tile), bf16),
                vmem((3, tasks, tile, tile), bf16),
                vmem((5, tasks, tile, tile), bf16),
                vmem((5, PARTS, tasks, rows, tile), bf16),
                vmem((PARTS, 8, tile), jnp.int32),
                vmem((tasks, rows, tile), f32),
                vmem((PARTS, slots, rows, tile), f32),
                vmem((PARTS, slots, rows, tile), bf16),
                vmem((PARTS, slots, rows, tile), bf16),
                vmem((tile, tile), f32),
                dma((2, tasks)),
                dma((tasks, 4)),
                dma((3, tasks)),
                dma((3, tasks)),
                dma((5, PARTS, tasks)),
                dma((5, PARTS, tasks)),
                dma((PARTS,)),
                dma((PARTS,)),
                dma((PARTS, slots)),
                dma((PARTS, slots)),
            ],
            compiler_params=pltpu.CompilerParams(
                collective_id=0, has_side_effects=True, vmem_limit_bytes=62 << 20
            ),
            name="ladder",
        )(task_count, task_target, fit_left, fit_right, t2_tiles)

    placed = (
        P("owner", "aux", None, None),
        P("owner", "aux", None, None),
        P("owner", None, None, None),
        P("owner"),
        P("owner"),
    )
    return jax.shard_map(
        on_device,
        mesh=mesh,
        in_specs=placed,
        out_specs=P("owner", "aux", None, None),
        check_vma=False,
    )
```

time: 238 us -> 43.7 us (0.18)
  waiting for transfers between devices: 203 us -> 0 us
  Pallas kernels: 0 us -> 41.5 us
  between operations: 13.5 us -> 0.66 us
  matrix products: 11 us -> 0 us
  local copies, waits for them, and re-layouts: 6.69 us -> 1.38 us
    unnamed x3 -> x0, waiting for transfers between devices: 116 us -> none
    reduce_scatter x1 -> x0, waiting for transfers between devices: 86.7 us -> none  [on_device(): lax.psum_scatter(per_owner, 'owner', scatter_dimension=0, tiled=True)]
    pallas_call x0 -> x1, Pallas kernels: none -> 41.5 us  [on_device(): pl.pallas_call(functools.partial(kernel, (owners, aux, tasks, naux, tile)...]
    dot_general x2 -> x0, matrix products: 11 us -> none  [the longest x1 9.87 us: ladder_term(): jnp.einsum('qiad,qbd->iab', halves, right_fit, preferred_element_type=jnp...]
    dot_general x1 -> x0, local copies, waits for them, and re-layouts: 2.55 us -> none  [owner_sums(): jnp.einsum('nt,tpxy->npxy', one_hot, shares, precision=lax.Precision.HIGH...]
  transfers between devices with their start and end apart: 2 -> 0, of which waited for: 2 -> 0; matrix products, arithmetic and copies ran while one was open for 0% -> 0% of each run, Pallas kernels for 0% -> 0%
where the time goes in v2:
time: 43.7 us; the launch traced here: 43.5 us
  Pallas kernels  41.5 us (95%)
  local copies, waits for them, and re-layouts  1.38 us (3%)
  between operations  0.66 us (2%)
    pallas_call x1, Pallas kernels, on_device(): pl.pallas_call(functools.partial(kernel, (owners, aux, tasks, naux, tile)...  41.5 us
    unnamed x1, local copies, waits for them, and re-layouts  1.38 us

profile of v2, /device:TPU:1, one launch (start us, length us, event | category | flops | bytes accessed | tf_op | source)
XLA Modules:
  0.0 43.5 jit_solution(11224748335991568824)
XLA Ops:
  0.7 41.5 %ladder.1 = bf16[1,1,128,128]{3,2,1,0:T(8,128)(2,1)} custom-call(s32[1]{0:T(128)S(6)} %copy.7.count_ref, s32[4]{0:T(128)} %target_ref.1, bf16[4,32,128,128]{3,2,1,0:T(8,128)(2,1)} %left_hbm.1, bf16[4,32,128,128]{3,2,1,0:T(8,128)(2,1)} %right_hbm.1, bf16[4,8,128,128]{3,2,1,0:T(8,128)(2,1)} %t2_hbm.1), custom_call_target="tpu_custom_call" | custom-call | tf_op jit(solution)/shard_map/ladder/pallas_call | solution.py:348
  42.1 1.4 %copy.8 = bf16[1,1,128,128]{3,2,1,0:T(8,128)(2,1)} copy(bf16[1,1,128,128]{3,2,1,0:T(8,128)(2,1)} %ladder.1) | data formatting | bytes 65536

commit v3 on v2

--- a/solution.py
+++ b/solution.py
@@ -12,7 +12,6 @@
 SIDE, CORES, PARTS, CHUNK = 4, 2, 4, 4
 OFFSETS = ((4, 3), (5, 1), (2, 6), (7, 0))
 NEAR_DZ = (1, 2, 6, 7, 0)
-HOLD = 2
 
 
 def kernel(
@@ -105,17 +104,8 @@
             recv_sem=block_recv.at[m, k], device_id=(owner_at(m, k), z), device_id_type=MESH,
         )
 
-    def place(u):
-        late, i = u // (2 * tasks), lax.rem(u, 2 * tasks)
-        last, j = i // tasks, lax.rem(i, tasks)
-        g_late = (1 - last) * (i // 2) + last * (2 + lax.rem(j, 2))
-        stage_late = (1 - last) * (3 - lax.rem(i, 2)) + last * (2 + j // 2)
-        g = (1 - late) * (u // 2) + late * g_late
-        stage = (1 - late) * lax.rem(u, 2) + late * stage_late
-        return g, stage
-
     def amplitudes(u):
-        g, stage = place(u)
+        g, stage = lax.rem(u, tasks), u // tasks
         found = []
         for p in range(2):
             a, b, c, d = (pair[p] for pair in OFFSETS)
@@ -126,7 +116,7 @@
         return jnp.concatenate(found, axis=0)
 
     def first(half, u, amps, q):
-        g, _ = place(u)
+        g = lax.rem(u, tasks)
         block = lax.dot_general(
             amps, left[g, pl.ds(q, CHUNK)].reshape(CHUNK * tile, tile), (((1,), (1,)), ((), ())),
             preferred_element_type=f32,
@@ -138,7 +128,7 @@
                 ]
 
     def second(half, u, q):
-        g, _ = place(u)
+        g = lax.rem(u, tasks)
         fit = jnp.concatenate([right[g, q + k] for k in range(CHUNK)], axis=1)
         value = jnp.dot(fit, half[q * tile : (q + CHUNK) * tile, :], preferred_element_type=f32)
         if q == 0:
@@ -146,54 +136,60 @@
         else:
             term[...] += value
 
+    def wait_first(u):
+        @pl.when(u < tasks)
+        def _():
+            load_t2(u).wait()
+            for k in range(4):
+                load_left(u, k).wait()
+
+    def wait_second(u):
+        @pl.when(u < tasks)
+        def _():
+            load_right(u).wait()
+
     def multiply(half_new, half_old, u):
+        wait_first(u + 1)
+
+        @pl.when(u < tasks - 2)
+        def _():
+            start_loads(u + 2)
+
+        wait_second(u)
         amps = amplitudes(u + 1)
         for q in range(0, naux, CHUNK):
             first(half_new, u + 1, amps, q)
             second(half_old, u, q)
 
-    def send(u, carry):
-        g, stage = place(u)
+    def send_near(s, g, value):
+        near_out[s, g] = value.astype(bf16)
+        for m in range(PARTS):
+            if s < 4 or m:
+                near_copy(s, m, g).start()
+
+    def send_relay(p, g, value):
+        far_out[p, g] = value.astype(bf16)
+        relay_copy(p, g).start()
+
+    def deliver(u):
+        g, stage = lax.rem(u, tasks), u // tasks
+        lower, upper = slice(0, tile), slice(tile, 2 * tile)
+
+        @pl.when(u == 0)
+        def _():
+            pl.semaphore_wait(barrier, 4 * PARTS + owners - 1)
+            for m in range(1, PARTS):
+                info_copy(m).start()
 
         @pl.when(stage == 0)
         def _():
-            relay_copy(0, g).start()
-            relay_copy(1, g).start()
+            send_relay(0, g, term[:, lower])
+            send_relay(1, g, term[:, upper])
 
         @pl.when(stage == 1)
         def _():
-            relay_copy(2, g).start()
-            for m in range(PARTS):
-                near_copy(0, m, g).start()
-
-        @pl.when(stage == 2)
-        def _():
-            for m in range(PARTS):
-                near_copy(1, m, g).start()
-                near_copy(2, m, g).start()
-
-        @pl.when(stage == 3)
-        def _():
-            for m in range(PARTS):
-                near_copy(3, m, g).start()
-            for m in range(1, PARTS):
-                near_copy(4, m, g).start()
-
-        return carry
-
-    def deliver(u):
-        g, stage = place(u)
-        lower, upper = slice(0, tile), slice(tile, 2 * tile)
-
-        @pl.when(stage == 0)
-        def _():
-            far_out[0, g] = term[:, lower].astype(bf16)
-            far_out[1, g] = term[:, upper].astype(bf16)
-
-        @pl.when(stage == 1)
-        def _():
-            far_out[2, g] = term[:, lower].astype(bf16)
-            near_out[0, g] = term[:, upper].astype(bf16)
+            send_relay(2, g, term[:, lower])
+            send_near(0, g, term[:, upper])
 
         @pl.when(stage == 2)
         def _():
@@ -201,47 +197,18 @@
                 relay_copy(p, g).wait_recv()
             extra = relay[0, g].astype(f32)
             up = (lax.rem(g, 2) == 0).astype(f32)
-            near_out[1, g] = (term[:, lower] + relay[1, g].astype(f32) + extra * up).astype(bf16)
-            near_out[2, g] = (term[:, upper] + relay[2, g].astype(f32) + extra * (1.0 - up)).astype(bf16)
+            send_near(1, g, term[:, lower] + relay[1, g].astype(f32) + extra * up)
+            send_near(2, g, term[:, upper] + relay[2, g].astype(f32) + extra * (1.0 - up))
 
         @pl.when(stage == 3)
         def _():
-            near_out[3, g] = term[:, lower].astype(bf16)
-            near_out[4, g] = term[:, upper].astype(bf16)
+            send_near(3, g, term[:, lower])
+            send_near(4, g, term[:, upper])
             own[g] = term[pl.ds(pl.multiple_of(part * rows, rows), rows), upper]
 
-        if isinstance(u, int):
-            send(u, 0)
-        else:
-            @pl.when(u == HOLD)
-            def _():
-                pl.semaphore_wait(barrier, 4 * PARTS + owners - 1)
-                for m in range(1, PARTS):
-                    info_copy(m).start()
-                lax.fori_loop(0, HOLD, send, 0)
-
-            @pl.when(u >= HOLD)
-            def _():
-                send(u, 0)
-
     def pair_of_units(v, carry):
-        @pl.when(v < tasks)
-        def _():
-            load_right(v).wait()
-
         multiply(half_odd, half_even, 2 * v)
         deliver(2 * v)
-
-        @pl.when(v < tasks - 1)
-        def _():
-            load_t2(v + 1).wait()
-            for k in range(4):
-                load_left(v + 1, k).wait()
-
-        @pl.when(v < tasks - 2)
-        def _():
-            start_loads(v + 2)
-
         multiply(half_even, half_odd, 2 * v + 1)
         deliver(2 * v + 1)
         return carry

time: 43.7 us -> 43.1 us (0.986)
  Pallas kernels: 41.5 us -> 40.8 us
    pallas_call x1, Pallas kernels: 41.5 us -> 40.8 us  [on_device(): pl.pallas_call(functools.partial(kernel, (owners, aux, tasks, naux, tile)...]
where the time goes in v3:
time: 43.1 us; the launch traced here: 42.9 us
  Pallas kernels  40.8 us (95%)
  local copies, waits for them, and re-layouts  1.38 us (3%)
  between operations  0.66 us (2%)
    pallas_call x1, Pallas kernels, on_device(): pl.pallas_call(functools.partial(kernel, (owners, aux, tasks, naux, tile)...  40.8 us
    unnamed x1, local copies, waits for them, and re-layouts  1.38 us

profile of v3, /device:TPU:1, one launch (start us, length us, event | category | flops | bytes accessed | tf_op | source)
XLA Modules:
  0.0 42.9 jit_solution(3062638879506365300)
XLA Ops:
  0.7 40.8 %ladder.1 = bf16[1,1,128,128]{3,2,1,0:T(8,128)(2,1)} custom-call(s32[1]{0:T(128)S(6)} %copy.7.count_ref, s32[4]{0:T(128)} %target_ref.1, bf16[4,32,128,128]{3,2,1,0:T(8,128)(2,1)} %left_hbm.1, bf16[4,32,128,128]{3,2,1,0:T(8,128)(2,1)} %right_hbm.1, bf16[4,8,128,128]{3,2,1,0:T(8,128)(2,1)} %t2_hbm.1), custom_call_target="tpu_custom_call" | custom-call | tf_op jit(solution)/shard_map/ladder/pallas_call | solution.py:315
  41.5 1.4 %copy.8 = bf16[1,1,128,128]{3,2,1,0:T(8,128)(2,1)} copy(bf16[1,1,128,128]{3,2,1,0:T(8,128)(2,1)} %ladder.1) | data formatting | bytes 65536

commit v4 on v3

--- a/solution.py
+++ b/solution.py
@@ -50,13 +50,11 @@
         part_of = pl.ds(k * (naux // 4), naux // 4)
         return pltpu.make_async_copy(left_hbm.at[g, part_of], left.at[g, part_of], left_sem.at[g, k])
 
-    def start_loads(g):
+    for g in range(tasks):
         load_t2(g).start()
         for k in range(4):
             load_left(g, k).start()
         load_right(g).start()
-
-    start_loads(0)
 
     barrier = pltpu.get_barrier_semaphore()
     for dz in (1, 2, 6, 7):
@@ -150,11 +148,6 @@
 
     def multiply(half_new, half_old, u):
         wait_first(u + 1)
-
-        @pl.when(u < tasks - 2)
-        def _():
-            start_loads(u + 2)
-
         wait_second(u)
         amps = amplitudes(u + 1)
         for q in range(0, naux, CHUNK):
@@ -218,8 +211,6 @@
     for q in range(0, naux, CHUNK):
         if q % (naux // 4) == 0:
             load_left(0, q // (naux // 4)).wait()
-        if q == naux - naux // 4:
-            start_loads(1)
         first(half_even, 0, amps, q)
     lax.fori_loop(0, units // 2 - 1, pair_of_units, 0)
     multiply(half_odd, half_even, units - 2)

time: 43.1 us -> 42.6 us (0.988)
    pallas_call x1, Pallas kernels: 40.8 us -> 40.4 us  [on_device(): pl.pallas_call(functools.partial(kernel, (owners, aux, tasks, naux, tile)...]
where the time goes in v4:
time: 42.6 us; the launch traced here: 42.4 us
  Pallas kernels  40.4 us (95%)
  local copies, waits for them, and re-layouts  1.38 us (3%)
  between operations  0.66 us (2%)
    pallas_call x1, Pallas kernels, on_device(): pl.pallas_call(functools.partial(kernel, (owners, aux, tasks, naux, tile)...  40.4 us
    unnamed x1, local copies, waits for them, and re-layouts  1.38 us

profile of v4, /device:TPU:1, one launch (start us, length us, event | category | flops | bytes accessed | tf_op | source)
XLA Modules:
  0.0 42.4 jit_solution(8281545116503020610)
XLA Ops:
  0.7 40.4 %ladder.1 = bf16[1,1,128,128]{3,2,1,0:T(8,128)(2,1)} custom-call(s32[1]{0:T(128)S(6)} %copy.7.count_ref, s32[4]{0:T(128)} %target_ref.1, bf16[4,32,128,128]{3,2,1,0:T(8,128)(2,1)} %left_hbm.1, bf16[4,32,128,128]{3,2,1,0:T(8,128)(2,1)} %right_hbm.1, bf16[4,8,128,128]{3,2,1,0:T(8,128)(2,1)} %t2_hbm.1), custom_call_target="tpu_custom_call" | custom-call | tf_op jit(solution)/shard_map/ladder/pallas_call | solution.py:306
  41.0 1.4 %copy.8 = bf16[1,1,128,128]{3,2,1,0:T(8,128)(2,1)} copy(bf16[1,1,128,128]{3,2,1,0:T(8,128)(2,1)} %ladder.1) | data formatting | bytes 65536

commit v5 on v4

--- a/solution.py
+++ b/solution.py
@@ -12,6 +12,7 @@
 SIDE, CORES, PARTS, CHUNK = 4, 2, 4, 4
 OFFSETS = ((4, 3), (5, 1), (2, 6), (7, 0))
 NEAR_DZ = (1, 2, 6, 7, 0)
+HOLD = 2
 
 
 def kernel(
@@ -168,16 +169,24 @@
         g, stage = lax.rem(u, tasks), u // tasks
         lower, upper = slice(0, tile), slice(tile, 2 * tile)
 
-        @pl.when(u == 0)
+        @pl.when(u == HOLD)
         def _():
             pl.semaphore_wait(barrier, 4 * PARTS + owners - 1)
             for m in range(1, PARTS):
                 info_copy(m).start()
+            for held in range(HOLD):
+                relay_copy(0, held).start()
+                relay_copy(1, held).start()
 
         @pl.when(stage == 0)
         def _():
-            send_relay(0, g, term[:, lower])
-            send_relay(1, g, term[:, upper])
+            far_out[0, g] = term[:, lower].astype(bf16)
+            far_out[1, g] = term[:, upper].astype(bf16)
+
+            @pl.when(u >= HOLD)
+            def _():
+                relay_copy(0, g).start()
+                relay_copy(1, g).start()
 
         @pl.when(stage == 1)
         def _():

time: 42.6 us -> 42.8 us (level)
  no operation moved by 1% of the time
where the time goes in v5:
time: 42.8 us; the launch traced here: 42.6 us
  Pallas kernels  40.6 us (95%)
  local copies, waits for them, and re-layouts  1.38 us (3%)
  between operations  0.66 us (2%)
    pallas_call x1, Pallas kernels, on_device(): pl.pallas_call(functools.partial(kernel, (owners, aux, tasks, naux, tile)...  40.6 us
    unnamed x1, local copies, waits for them, and re-layouts  1.38 us

profile of v5, /device:TPU:1, one launch (start us, length us, event | category | flops | bytes accessed | tf_op | source)
XLA Modules:
  0.0 42.6 jit_solution(16659429188753460404)
XLA Ops:
  0.7 40.6 %ladder.1 = bf16[1,1,128,128]{3,2,1,0:T(8,128)(2,1)} custom-call(s32[1]{0:T(128)S(6)} %copy.7.count_ref, s32[4]{0:T(128)} %target_ref.1, bf16[4,32,128,128]{3,2,1,0:T(8,128)(2,1)} %left_hbm.1, bf16[4,32,128,128]{3,2,1,0:T(8,128)(2,1)} %right_hbm.1, bf16[4,8,128,128]{3,2,1,0:T(8,128)(2,1)} %t2_hbm.1), custom_call_target="tpu_custom_call" | custom-call | tf_op jit(solution)/shard_map/ladder/pallas_call | solution.py:315
  41.2 1.4 %copy.8 = bf16[1,1,128,128]{3,2,1,0:T(8,128)(2,1)} copy(bf16[1,1,128,128]{3,2,1,0:T(8,128)(2,1)} %ladder.1) | data formatting | bytes 65536
